TPU v7x, 32 devices: a whole 2x2x4 slice. The times are simulated.
32 devices in a mesh: dp: 32 (over z, y, x, core), tensor: 1.
Axes of the slice: x: 2, y: 2, z: 4, core: 2. Of those that a mesh axis runs over, the one named last changes fastest.
Arguments:
- activations: bfloat16 [8192, 14336], P('dp', 'tensor'), may hold values from -6 to 6
- out_grads: bfloat16 [8192, 4096], P('dp', 'tensor'), may hold values from -0.06591797 to 0.06591797
Outputs:
- fisher: float32 [14336, 4096], P('tensor', 'dp')
All inputs are finite; a program needn't handle non-finite values.
Results may differ from a plain program's by a relative error of at most 0.0003.
Values may be sent and summed in bfloat16 or wider, within the bound.
A program may use at most 896 MiB of HBM per device.

v0:
```python
import jax
import jax.numpy as jnp
from jax import lax
from jax.sharding import PartitionSpec as P

LEN = 128


def per_device(activations, out_grads):
    gathered = lax.all_gather(out_grads, "tensor", axis=1, tiled=True)
    seq_count = activations.shape[0] // LEN
    features = activations.shape[1]
    inputs_seq = activations.reshape(seq_count, LEN, features)
    grads_seq = gathered.reshape(seq_count, LEN, gathered.shape[1])
    owned_cols = gathered.shape[1] // lax.axis_size("dp")

    def add_sequence(total, pair):
        grads = jnp.dot(pair[0].T, pair[1], preferred_element_type=jnp.float32)
        return (total + grads * grads, None)

    start_total = jnp.zeros((owned_cols * lax.axis_size("dp"), features), jnp.float32)
    total, unused = lax.scan(add_sequence, start_total, (grads_seq, inputs_seq))
    owned = lax.psum_scatter(total, "dp", scatter_dimension=0, tiled=True)
    return owned.T


def solution(mesh):
    in_specs = (P("dp", "tensor"), P("dp", "tensor"))
    out_specs = P("tensor", "dp")
    return jax.shard_map(
        per_device, mesh=mesh, in_specs=in_specs, out_specs=out_specs, check_vma=False
    )
```

profile of v0, /device:TPU:0, one launch (start us, length us, event | category | flops | bytes accessed | tf_op | source)
XLA Modules:
  0.0 2917.2 jit_solution(13677763645880863891)
XLA Ops:
  6.5 0.0 reduce-scatter.2.cloned.1.call-start
  6.5 229.9 %while.11 = (s32[]{:T(128)}, f32[4096,14336]{1,0:T(8,128)}, bf16[2,128,4096]{2,1,0:T(8,128)(2,1)}, bf16[2,128,14336]{2,1,0:T(8,128)(2,1)}, s32[]{:T(128)}, /*index=5*/s32[]{:T(128)}) while((s32[]{:T(128)}, f32[4096,14336]{1,0:T(8,128)}, bf16[2,128,4096]{2,1,0:T(8,128)(2,1)}, bf16[2,128,14336]{2,1,0:T(8,128)(2,1)}, s32[]{:T(128)}, ...), condition=%wide.region_1.2_spmd.clone, body=%wide.region_0.1_spmd.clone.sunk | while | flops 15208546304 | bytes 474482240 | solution.py:22
  6.5 76.5 %select_add_fusion.2 = f32[4096,14336]{1,0:T(8,128)} fusion(f32[4096,14336]{1,0:T(8,128)} %get-tuple-element.83, pred[]{:T(512)S(6)} %compare.3, bf16[2,128,14336]{2,1,0:T(8,128)(2,1)} %get-tuple-element.91, s32[]{:T(128)S(6)} %copy.6, bf16[2,128,4096]{2,1,0:T(8,128)(2,1)} %get-tuple-element.90), kind=kOutput, calls=%fused_computation.clone.3 | convolution fusion | flops 15208546304 | bytes 474482176 | tf_op jit(solution)/shard_map/while/body/eval_jaxpr/dot_general | solution.py:18
  83.0 153.4 %select_add_fusion.2 = f32[4096,14336]{1,0:T(8,128)} fusion(f32[4096,14336]{1,0:T(8,128)} %get-tuple-element.83, pred[]{:T(512)S(6)} %compare.3, bf16[2,128,14336]{2,1,0:T(8,128)(2,1)} %get-tuple-element.91, s32[]{:T(128)S(6)} %copy.6, bf16[2,128,4096]{2,1,0:T(8,128)(2,1)} %get-tuple-element.90), kind=kOutput, calls=%fused_computation.clone.3 | convolution fusion | flops 15208546304 | bytes 474482176 | tf_op jit(solution)/shard_map/while/body/eval_jaxpr/dot_general | solution.py:18
  236.4 228.2 %copy.3 = f32[4096,14336]{0,1:T(8,128)} copy(f32[4096,14336]{1,0:T(8,128)} %get-tuple-element.27) | data formatting | bytes 469762048 | tf_op jit(solution)/shard_map/while | solution.py:22
  464.6 0.0 reduce-scatter.2.cloned.1.call-update
  464.6 2445.7 %reduce-scatter.2.cloned.1.call-done = f32[128,14336]{0,1:T(8,128)} async-done(((f32[4096,14336]{0,1:T(8,128)}), f32[128,14336]{0,1:T(8,128)}) %reduce-scatter.2.cloned.1.call-update) | async-done | bytes 7340048 | tf_op jit(solution)/shard_map/reduce_scatter | solution.py:23
  (1 shorter events, 0.0 us)
Async XLA Ops:
  6.5 2903.8 %reduce-scatter.2.cloned.1.call-start = ((), (), s32[]{:S(2)}) async-start(), calls=%async_computation.1 | async-start | bytes 242221056 | tf_op jit(solution)/shard_map/reduce_scatter | solution.py:23
Sparse Core Ops, SparseCore 0:
  464.7 2445.5 reduce-scatter.1
where the time goes:
time: 2930 us; the launch traced here: 2920 us
  waiting for transfers between devices  2450 us (84%)
  matrix products  230 us (8%)
  local copies, waits for them, and re-layouts  228 us (8%)
    reduce_scatter x1, waiting for transfers between devices, per_device(): owned = lax.psum_scatter(total, 'dp', scatter_dimension=0, tiled=True)  2450 us
    dot_general x2, matrix products, add_sequence(): grads = jnp.dot(pair[0].T, pair[1], preferred_element_type=jnp.float32)  230 us
    while x1, local copies, waits for them, and re-layouts, per_device(): total, unused = lax.scan(add_sequence, start_total, (grads_seq, inputs_seq))  228 us
  transfers between devices with their start and end apart: 1, of which 1 were waited for; matrix products, arithmetic and copies ran while one was open for 0% of the time, Pallas kernels for 0%

commit v1 on v0

v1 whole, which is shorter than its diff:
```python
import functools

import jax
import jax.numpy as jnp
from jax import lax
from jax.experimental import pallas as pl
from jax.experimental.pallas import tpu as pltpu
from jax.sharding import PartitionSpec as P

LEN = 128
TILE_F = 256
TILE_D = 512
VMEM_BYTES = 48 * 1024 * 1024


def squares_kernel(near_ref, far_ref, grads_ref, out_ref, turned):
    seqs = near_ref.shape[0]
    tile_d = out_ref.shape[0] * out_ref.shape[2]
    owned = out_ref.shape[2]

    @pl.when(pl.program_id(1) == 0)
    def turn():
        for s in range(seqs):
            turned[2 * s] = near_ref[s].T
            turned[2 * s + 1] = far_ref[s].T

    start = pl.multiple_of(pl.program_id(1) * tile_d, tile_d)
    for half in range(tile_d // 256):
        total = jnp.zeros((turned.shape[1], 256), jnp.float32)
        for s in range(2 * seqs):
            grads = jnp.dot(
                turned[s],
                grads_ref[s, :, pl.ds(start + half * 256, 256)],
                preferred_element_type=jnp.float32,
            )
            total = total + grads * grads
        for j in range(256 // owned):
            out_ref[half * (256 // owned) + j] = total[:, j * owned:(j + 1) * owned]


def squares(near, far, grads, owned):
    seqs, _, f = near.shape
    d = grads.shape[2]
    inputs = pl.BlockSpec((seqs, LEN, TILE_F), lambda i, j: (0, 0, i))
    return pl.pallas_call(
        squares_kernel,
        grid=(f // TILE_F, d // TILE_D),
        in_specs=[inputs, inputs, pl.BlockSpec((2 * seqs, LEN, d), lambda i, j: (0, 0, 0))],
        out_specs=pl.BlockSpec((TILE_D // owned, TILE_F, owned), lambda i, j: (j, i, 0)),
        out_shape=jax.ShapeDtypeStruct((d // owned, f, owned), jnp.float32),
        scratch_shapes=[pltpu.VMEM((2 * seqs, TILE_F, LEN), jnp.bfloat16)],
        compiler_params=pltpu.CompilerParams(vmem_limit_bytes=VMEM_BYTES),
        cost_estimate=pl.CostEstimate(
            flops=2 * 2 * seqs * LEN * f * d,
            bytes_accessed=2 * 2 * seqs * LEN * (f + d) + 4 * f * d,
            transcendentals=0,
        ),
    )(near, far, grads)


def scattered(activations, gathered, n):
    seqs, f = activations.shape[0] // LEN, activations.shape[1]
    a = activations.reshape(seqs, LEN, f)
    g = gathered.reshape(seqs, LEN, gathered.shape[1])
    total = 0.0
    for s in range(seqs):
        grads = jnp.dot(g[s].T, a[s], preferred_element_type=jnp.float32)
        total = total + grads * grads
    return lax.psum_scatter(total, "dp", scatter_dimension=0, tiled=True).T


def per_device(n, activations, out_grads):
    gathered = lax.all_gather(out_grads, "tensor", axis=1, tiled=True)
    rows, f = activations.shape
    d = gathered.shape[1]
    owned = d // n
    inner, lo = 8, 2
    hi = n // (inner * lo)
    tiles = f // (inner * TILE_F)
    if n % (inner * lo) or f % (inner * TILE_F) or owned != 128:
        return scattered(activations, gathered, n)

    me = lax.axis_index("dp")
    h, l = me // (inner * lo), (me // inner) % lo
    groups = [[k * inner + i for i in range(inner)] for k in range(n // inner)]
    swap_lo = [(k, k ^ inner) for k in range(n)]
    step = inner * lo

    with jax.named_scope("grads_exchange"):
        g = gathered.reshape(rows, hi, lo, inner * owned)
        mine = lax.dynamic_index_in_dim(g, l, 2, keepdims=False)
        theirs = lax.dynamic_index_in_dim(g, 1 - l, 2, keepdims=False)
        got = lax.ppermute(theirs, "dp", swap_lo)
        both = jnp.stack([mine, got])
        seqs = rows // LEN
        cols = []
        for shift in list(range(1, hi)) + [0]:
            part = lax.dynamic_index_in_dim(both, (h + shift) % hi, 2, keepdims=False)
            part = part.reshape(2, seqs, LEN, inner * owned).transpose(1, 0, 2, 3)
            part = lax.all_gather(part, "dp", axis_index_groups=groups)
            cols.append(part.reshape(inner * seqs * 2, LEN, inner * owned))

    sizes = [1] + [2] * ((tiles - 1) // 2) + [1] * ((tiles - 1) % 2)
    wide = f // inner
    a = activations.reshape(rows, inner, wide)
    pieces = []
    first = 0
    for size in sizes:
        chunk = a[:, :, first * TILE_F:(first + size) * TILE_F].transpose(1, 0, 2)
        first += size
        with jax.named_scope("inputs_exchange"):
            near = lax.all_to_all(chunk, "dp", 0, 0, axis_index_groups=groups, tiled=True)
            near = near.reshape(inner * seqs, LEN, size * TILE_F)
            far = lax.ppermute(near, "dp", swap_lo)
        arrived = []
        for shift in range(1, hi):
            part = squares(near, far, cols[shift - 1], owned)
            pairs = [(k, (k + shift * step) % n) for k in range(n)]
            arrived.append(lax.ppermute(part, "dp", pairs))
        total = squares(near, far, cols[-1], owned)
        for part in arrived:
            total = total + part
        with jax.named_scope("to_owners"):
            pieces.append(lax.all_to_all(total, "dp", 0, 0, axis_index_groups=groups, tiled=True))
    return jnp.concatenate(pieces, axis=1).reshape(f, owned)


def solution(mesh):
    in_specs = (P("dp", "tensor"), P("dp", "tensor"))
    out_specs = P("tensor", "dp")
    body = functools.partial(per_device, mesh.shape["dp"])
    return jax.shard_map(
        body, mesh=mesh, in_specs=in_specs, out_specs=out_specs, check_vma=False
    )
```

time: 2930 us -> 598 us (0.20)
  waiting for transfers between devices: 2450 us -> 329 us
  matrix products: 230 us -> 0 us
  local copies, waits for them, and re-layouts: 228 us -> 45.6 us
  Pallas kernels: 0 us -> 109 us
  starting transfers between devices: 0.01 us -> 45.6 us
  blocking collectives: 0 us -> 30.4 us
    reduce_scatter x1 -> x0, waiting for transfers between devices: 2450 us -> none  [per_device(): owned = lax.psum_scatter(total, 'dp', scatter_dimension=0, tiled=True)]
    dot_general x2 -> x0, matrix products: 230 us -> none  [add_sequence(): grads = jnp.dot(pair[0].T, pair[1], preferred_element_type=jnp.float32)]
    while x1 -> x0, local copies, waits for them, and re-layouts: 228 us -> none  [per_device(): total, unused = lax.scan(add_sequence, start_total, (grads_seq, inputs_seq))]
    ppermute x0 -> x9, waiting for transfers between devices: none -> 227 us  [the longest x4 204 us: per_device(): arrived.append(lax.ppermute(part, 'dp', pairs))]
    pallas_call x0 -> x8, Pallas kernels: none -> 109 us  [squares(): pl.pallas_call(squares_kernel, grid=(f // TILE_F, d // TILE_D), in_specs=...]
    all_to_all x0 -> x7, waiting for transfers between devices: none -> 101 us  [the longest x4 101 us: per_device(): lax.all_to_all(chunk, 'dp', 0, 0, axis_index_groups=groups, tiled=True)]
    all_to_all x0 -> x1, blocking collectives: none -> 30.4 us  [per_device(): lax.all_to_all(total, 'dp', 0, 0, axis_index_groups=groups, tiled=True)]
    all_to_all x0 -> x7, starting transfers between devices: none -> 29.6 us  [the longest x4 17.2 us: per_device(): lax.all_to_all(chunk, 'dp', 0, 0, axis_index_groups=groups, tiled=True)]
  transfers between devices with their start and end apart: 1 -> 18, of which waited for: 1 -> 9; matrix products, arithmetic and copies ran while one was open for 0% -> 8% of each run, Pallas kernels for 0% -> 18%
where the time goes in v1:
time: 598 us; the launch traced here: 592 us
  waiting for transfers between devices  329 us (55%)
  Pallas kernels  109 us (18%)
  starting transfers between devices  45.6 us (8%)
  local copies, waits for them, and re-layouts  45.6 us (8%)
  blocking collectives  30.4 us (5%)
  other arithmetic  17.6 us (3%)
  between operations  14 us (2%)
    ppermute x4, waiting for transfers between devices, per_device(): arrived.append(lax.ppermute(part, 'dp', pairs))  204 us
    pallas_call x8, Pallas kernels, squares(): pl.pallas_call(squares_kernel, grid=(f // TILE_F, d // TILE_D), in_specs=...  109 us
    all_to_all x4, waiting for transfers between devices, per_device(): lax.all_to_all(chunk, 'dp', 0, 0, axis_index_groups=groups, tiled=True)  101 us
    all_to_all x1, blocking collectives, per_device(): lax.all_to_all(total, 'dp', 0, 0, axis_index_groups=groups, tiled=True)  30.4 us
    ppermute x1, waiting for transfers between devices, per_device(): got = lax.ppermute(theirs, 'dp', swap_lo)  22.8 us
    unnamed x8, local copies, waits for them, and re-layouts  20.4 us
    all_to_all x4, starting transfers between devices, per_device(): lax.all_to_all(chunk, 'dp', 0, 0, axis_index_groups=groups, tiled=True)  17.2 us
    all_gather x2, local copies, waits for them, and re-layouts, per_device(): part = lax.all_gather(part, 'dp', axis_index_groups=groups)  16.4 us
  transfers between devices with their start and end apart: 18, of which 9 were waited for; matrix products, arithmetic and copies ran while one was open for 8% of the time, Pallas kernels for 18%

profile of v1, /device:TPU:0, one launch (start us, length us, event | category | flops | bytes accessed | tf_op | source)
XLA Modules:
  0.0 591.6 jit_solution(77367650749922352)
XLA Ops:
  6.5 3.3 copy.14
  16.8 22.8 %collective-permute-done.1 = bf16[256,2,1024]{2,0,1:T(8,128)(2,1)S(1)} collective-permute-done((bf16[256,2,1024]{2,0,1:T(8,128)(2,1)}, bf16[256,2,1024]{2,0,1:T(8,128)(2,1)S(1)}, u32[]{:S(2)}, u32[]{:S(2)}) %collective-permute-start.1) | collective-permute-done | bytes 1048608 | tf_op jit(solution)/shard_map/grads_exchange/ppermute | solution.py:93
  41.9 5.2 copy.26
  51.4 3.9 all-to-all-start
  55.3 4.8 fusion.2
  62.1 14.5 %all-to-all-done = bf16[8,256,256]{2,1,0:T(8,128)(2,1)S(1)} async-done(((bf16[8,256,256]{2,1,0:T(8,128)(2,1)}), bf16[8,256,256]{2,1,0:T(8,128)(2,1)S(1)}, u32[]{:S(2)}, u32[]{:S(2)}) %all-to-all-start) | async-done | bytes 1048608 | tf_op jit(solution)/shard_map/inputs_exchange/all_to_all | solution.py:112
  76.6 4.4 all-to-all-start.6
  83.0 46.8 %all-to-all-done.6 = bf16[8,256,512]{2,1,0:T(8,128)(2,1)} async-done(((bf16[8,256,512]{2,1,0:T(8,128)(2,1)}), bf16[8,256,512]{2,1,0:T(8,128)(2,1)}, u32[]{:S(2)}, u32[]{:S(2)}) %all-to-all-start.6) | async-done | bytes 2097184 | tf_op jit(solution)/shard_map/inputs_exchange/all_to_all | solution.py:112
  129.8 4.4 all-to-all-start.4
  136.3 3.6 copy.33
  139.9 32.1 %all-to-all-done.4 = bf16[8,256,512]{2,1,0:T(8,128)(2,1)} async-done(((bf16[8,256,512]{2,1,0:T(8,128)(2,1)}), bf16[8,256,512]{2,1,0:T(8,128)(2,1)}, u32[]{:S(2)}, u32[]{:S(2)}) %all-to-all-start.4) | async-done | bytes 2097184 | tf_op jit(solution)/shard_map/inputs_exchange/all_to_all | solution.py:112
  172.0 4.5 all-to-all-start.2
  178.1 8.2 %copy.18 = bf16[16,2,128,1024]{3,2,1,0:T(8,128)(2,1)} copy(bf16[16,2,128,1024]{3,2,0,1:T(8,128)(2,1)} %all-gather.7.cloned.1.call-done) | data formatting | bytes 16777216 | tf_op jit(solution)/shard_map/grads_exchange/all_gather | solution.py:100
  186.4 15.7 %shard_map.35 = f32[8,512,128]{2,1,0:T(8,128)} custom-call(bf16[16,128,512]{2,1,0:T(8,128)(2,1)} %bitcast.17.near_ref, bf16[16,128,512]{2,1,0:T(8,128)(2,1)} %collective-permute-done.7.far_ref, bf16[32,128,1024]{2,1,0:T(8,128)(2,1)} %bitcast.34), custom_call_target="tpu_custom_call" | custom-call | flops 4294967296 | bytes 14680064 | tf_op jit(solution)/shard_map/pallas_call | solution.py:45
  205.4 8.9 %shard_map.29 = f32[8,256,128]{2,1,0:T(8,128)S(1)} custom-call(bf16[16,128,256]{2,1,0:T(8,128)(2,1)S(1)} %bitcast.32, bf16[16,128,256]{2,1,0:T(8,128)(2,1)S(1)} %collective-permute-done.far_ref, bf16[32,128,1024]{2,1,0:T(8,128)(2,1)} %bitcast.35), custom_call_target="tpu_custom_call" | custom-call | flops 2147483648 | bytes 11534336 | tf_op jit(solution)/shard_map/pallas_call | solution.py:45
  216.8 7.9 %all-to-all-done.2 = bf16[8,256,512]{2,1,0:T(8,128)(2,1)} async-done(((bf16[8,256,512]{2,1,0:T(8,128)(2,1)}), bf16[8,256,512]{2,1,0:T(8,128)(2,1)}, u32[]{:S(2)}, u32[]{:S(2)}) %all-to-all-start.2) | async-done | bytes 2097184 | tf_op jit(solution)/shard_map/inputs_exchange/all_to_all | solution.py:112
  226.1 8.2 %copy.17 = bf16[16,2,128,1024]{3,2,1,0:T(8,128)(2,1)} copy(bf16[16,2,128,1024]{3,2,0,1:T(8,128)(2,1)} %all-gather.5.cloned.1.call-done) | data formatting | bytes 16777216 | tf_op jit(solution)/shard_map/grads_exchange/all_gather | solution.py:100
  234.3 8.8 %shard_map.28 = f32[8,256,128]{2,1,0:T(8,128)S(1)} custom-call(bf16[16,128,256]{2,1,0:T(8,128)(2,1)S(1)} %bitcast.33, bf16[16,128,256]{2,1,0:T(8,128)(2,1)S(1)} %collective-permute-done.far_ref, bf16[32,128,1024]{2,1,0:T(8,128)(2,1)} %bitcast.38), custom_call_target="tpu_custom_call" | custom-call | flops 2147483648 | bytes 11534336 | tf_op jit(solution)/shard_map/pallas_call | solution.py:45
  243.1 98.0 %collective-permute-done.2 = f32[8,256,128]{2,1,0:T(8,128)} collective-permute-done((f32[8,256,128]{2,1,0:T(8,128)S(1)}, f32[8,256,128]{2,1,0:T(8,128)}, u32[]{:S(2)}, u32[]{:S(2)}) %collective-permute-start.2) | collective-permute-done | bytes 1048608 | tf_op jit(solution)/shard_map/ppermute | solution.py:119
  343.4 4.0 all-to-all-start.1
  347.4 15.0 %shard_map.33 = f32[8,512,128]{2,1,0:T(8,128)S(1)} custom-call(bf16[16,128,512]{2,1,0:T(8,128)(2,1)} %bitcast.15.near_ref, bf16[16,128,512]{2,1,0:T(8,128)(2,1)} %collective-permute-done.5.far_ref, bf16[32,128,1024]{2,1,0:T(8,128)(2,1)} %bitcast.36), custom_call_target="tpu_custom_call" | custom-call | flops 4294967296 | bytes 14680064 | tf_op jit(solution)/shard_map/pallas_call | solution.py:45
  362.5 15.0 %shard_map.34 = f32[8,512,128]{2,1,0:T(8,128)S(1)} custom-call(bf16[16,128,512]{2,1,0:T(8,128)(2,1)} %bitcast.17.near_ref, bf16[16,128,512]{2,1,0:T(8,128)(2,1)} %collective-permute-done.7.far_ref, bf16[32,128,1024]{2,1,0:T(8,128)(2,1)} %bitcast.39), custom_call_target="tpu_custom_call" | custom-call | flops 4294967296 | bytes 14680064 | tf_op jit(solution)/shard_map/pallas_call | solution.py:45
  377.5 3.1 add.53
  380.6 4.6 all-to-all-start.7
  385.2 15.7 %shard_map.31 = f32[8,512,128]{2,1,0:T(8,128)} custom-call(bf16[16,128,512]{2,1,0:T(8,128)(2,1)} %bitcast.13.near_ref, bf16[16,128,512]{2,1,0:T(8,128)(2,1)} %collective-permute-done.3.far_ref, bf16[32,128,1024]{2,1,0:T(8,128)(2,1)} %bitcast.37), custom_call_target="tpu_custom_call" | custom-call | flops 4294967296 | bytes 14680064 | tf_op jit(solution)/shard_map/pallas_call | solution.py:45
  403.8 15.0 %shard_map.32 = f32[8,512,128]{2,1,0:T(8,128)S(1)} custom-call(bf16[16,128,512]{2,1,0:T(8,128)(2,1)} %bitcast.15.near_ref, bf16[16,128,512]{2,1,0:T(8,128)(2,1)} %collective-permute-done.5.far_ref, bf16[32,128,1024]{2,1,0:T(8,128)(2,1)} %bitcast.40), custom_call_target="tpu_custom_call" | custom-call | flops 4294967296 | bytes 14680064 | tf_op jit(solution)/shard_map/pallas_call | solution.py:45
  418.8 82.6 %collective-permute-done.6 = f32[8,512,128]{2,1,0:T(8,128)} collective-permute-done((f32[8,512,128]{2,1,0:T(8,128)S(1)}, f32[8,512,128]{2,1,0:T(8,128)}, u32[]{:S(2)}, u32[]{:S(2)}) %collective-permute-start.6) | collective-permute-done | bytes 2097184 | tf_op jit(solution)/shard_map/ppermute | solution.py:119
  504.5 3.9 all-to-all-start.5
  508.4 15.0 %shard_map.30 = f32[8,512,128]{2,1,0:T(8,128)S(1)} custom-call(bf16[16,128,512]{2,1,0:T(8,128)(2,1)} %bitcast.13.near_ref, bf16[16,128,512]{2,1,0:T(8,128)(2,1)} %collective-permute-done.3.far_ref, bf16[32,128,1024]{2,1,0:T(8,128)(2,1)} %bitcast.41), custom_call_target="tpu_custom_call" | custom-call | flops 4294967296 | bytes 14680064 | tf_op jit(solution)/shard_map/pallas_call | solution.py:45
  523.4 22.9 %collective-permute-done.4 = f32[8,512,128]{2,1,0:T(8,128)} collective-permute-done((f32[8,512,128]{2,1,0:T(8,128)}, f32[8,512,128]{2,1,0:T(8,128)}, u32[]{:S(2)}, u32[]{:S(2)}) %collective-permute-start.4) | collective-permute-done | bytes 2097184 | tf_op jit(solution)/shard_map/ppermute | solution.py:119
  549.4 30.4 %all_to_all.40 = f32[8,512,128]{2,1,0:T(8,128)S(1)} all-to-all(f32[8,512,128]{2,1,0:T(8,128)} %add.51), channel_id=1, replica_groups={{0,1,2,3,4,5,6,7},{8,9,10,11,12,13,14,15},{16,17,18,19,20,21,22,23},{24..., dimensions={0} | all-to-all | bytes 4194304 | tf_op jit(solution)/shard_map/to_owners/all_to_all | solution.py:124
  579.9 4.5 pad_maximum_fusion
  (36 shorter events, 40.0 us)
Async XLA Ops:
  6.5 171.6 %all-gather.7.cloned.1.call-start = ((), (), s32[]{:S(2)}) async-start(), calls=%async_computation.9 | async-start | bytes 9437184 | tf_op jit(solution)/shard_map/grads_exchange/all_gather | solution.py:100
  13.2 26.4 %collective-permute-start.1 = (bf16[256,2,1024]{2,0,1:T(8,128)(2,1)}, bf16[256,2,1024]{2,0,1:T(8,128)(2,1)S(1)}, u32[]{:S(2)}, u32[]{:S(2)}) collective-permute-start(bf16[256,2,1024]{2,0,1:T(8,128)(2,1)} %bitcast.4), channel_id=1, source_target_pairs={{0,8},{1,9},{2,10},{3,11},{4,12},{5,13},{6,14},{7,15},{8,0},{9,1},... | collective-permute-start | bytes 3145736 | tf_op jit(solution)/shard_map/grads_exchange/ppermute | solution.py:93
  41.1 185.0 %all-gather.5.cloned.1.call-start = ((), (), s32[]{:S(2)}) async-start(), calls=%async_computation.8 | async-start | bytes 9437184 | tf_op jit(solution)/shard_map/grads_exchange/all_gather | solution.py:100
  47.1 3.1 copy-start
  51.4 25.2 %all-to-all-start = ((bf16[8,256,256]{2,1,0:T(8,128)(2,1)}), bf16[8,256,256]{2,1,0:T(8,128)(2,1)S(1)}, u32[]{:S(2)}, u32[]{:S(2)}) async-start(bf16[8,256,256]{2,1,0:T(8,128)(2,1)} %bitcast.30), calls=%async_computation | async-start | bytes 2097152 | tf_op jit(solution)/shard_map/inputs_exchange/all_to_all | solution.py:112
  76.6 53.3 %all-to-all-start.6 = ((bf16[8,256,512]{2,1,0:T(8,128)(2,1)}), bf16[8,256,512]{2,1,0:T(8,128)(2,1)}, u32[]{:S(2)}, u32[]{:S(2)}) async-start(bf16[8,256,512]{2,1,0:T(8,128)(2,1)} %bitcast.27), calls=%async_computation.6 | async-start | bytes 4194304 | tf_op jit(solution)/shard_map/inputs_exchange/all_to_all | solution.py:112
  129.8 42.2 %all-to-all-start.4 = ((bf16[8,256,512]{2,1,0:T(8,128)(2,1)}), bf16[8,256,512]{2,1,0:T(8,128)(2,1)}, u32[]{:S(2)}, u32[]{:S(2)}) async-start(bf16[8,256,512]{2,1,0:T(8,128)(2,1)} %bitcast.28), calls=%async_computation.4 | async-start | bytes 4194304 | tf_op jit(solution)/shard_map/inputs_exchange/all_to_all | solution.py:112
  134.2 52.2 %collective-permute-start.7 = (bf16[16,128,512]{2,1,0:T(8,128)(2,1)}, bf16[16,128,512]{2,1,0:T(8,128)(2,1)}, u32[]{:S(2)}, u32[]{:S(2)}) collective-permute-start(bf16[16,128,512]{2,1,0:T(8,128)(2,1)} %bitcast.17.near_ref), channel_id=1, source_target_pairs={{0,8},{1,9},{2,10},{3,11},{4,12},{5,13},{6,14},{7,15},{8,0},{9,1},... | collective-permute-start | bytes 6291464 | tf_op jit(solution)/shard_map/inputs_exchange/ppermute | solution.py:114
  135.7 69.6 %collective-permute-start = (bf16[16,128,256]{2,1,0:T(8,128)(2,1)S(1)}, bf16[16,128,256]{2,1,0:T(8,128)(2,1)S(1)}, u32[]{:S(2)}, u32[]{:S(2)}) collective-permute-start(bf16[16,128,256]{2,1,0:T(8,128)(2,1)S(1)} %bitcast.31), channel_id=1, source_target_pairs={{0,8},{1,9},{2,10},{3,11},{4,12},{5,13},{6,14},{7,15},{8,0},{9,1},... | collective-permute-start | bytes 3145736 | tf_op jit(solution)/shard_map/inputs_exchange/ppermute | solution.py:114
  172.0 52.6 %all-to-all-start.2 = ((bf16[8,256,512]{2,1,0:T(8,128)(2,1)}), bf16[8,256,512]{2,1,0:T(8,128)(2,1)}, u32[]{:S(2)}, u32[]{:S(2)}) async-start(bf16[8,256,512]{2,1,0:T(8,128)(2,1)} %bitcast.45), calls=%async_computation.2 | async-start | bytes 4194304 | tf_op jit(solution)/shard_map/inputs_exchange/all_to_all | solution.py:112
  176.6 170.8 %collective-permute-start.5 = (bf16[16,128,512]{2,1,0:T(8,128)(2,1)}, bf16[16,128,512]{2,1,0:T(8,128)(2,1)}, u32[]{:S(2)}, u32[]{:S(2)}) collective-permute-start(bf16[16,128,512]{2,1,0:T(8,128)(2,1)} %bitcast.15.near_ref), channel_id=1, source_target_pairs={{0,8},{1,9},{2,10},{3,11},{4,12},{5,13},{6,14},{7,15},{8,0},{9,1},... | collective-permute-start | bytes 6291464 | tf_op jit(solution)/shard_map/inputs_exchange/ppermute | solution.py:114
  202.0 175.4 %collective-permute-start.8 = (f32[8,512,128]{2,1,0:T(8,128)}, f32[8,512,128]{2,1,0:T(8,128)}, u32[]{:S(2)}, u32[]{:S(2)}) collective-permute-start(f32[8,512,128]{2,1,0:T(8,128)} %shard_map.35), channel_id=1, source_target_pairs={{0,16},{1,17},{2,18},{3,19},{4,20},{5,21},{6,22},{7,23},{8,24},{9,... | collective-permute-start | bytes 6291464 | tf_op jit(solution)/shard_map/ppermute | solution.py:119
  214.3 126.8 %collective-permute-start.2 = (f32[8,256,128]{2,1,0:T(8,128)S(1)}, f32[8,256,128]{2,1,0:T(8,128)}, u32[]{:S(2)}, u32[]{:S(2)}) collective-permute-start(f32[8,256,128]{2,1,0:T(8,128)S(1)} %shard_map.29), channel_id=1, source_target_pairs={{0,16},{1,17},{2,18},{3,19},{4,20},{5,21},{6,22},{7,23},{8,24},{9,... | collective-permute-start | bytes 3145736 | tf_op jit(solution)/shard_map/ppermute | solution.py:119
  224.6 160.6 %collective-permute-start.3 = (bf16[16,128,512]{2,1,0:T(8,128)(2,1)}, bf16[16,128,512]{2,1,0:T(8,128)(2,1)}, u32[]{:S(2)}, u32[]{:S(2)}) collective-permute-start(bf16[16,128,512]{2,1,0:T(8,128)(2,1)} %bitcast.13.near_ref), channel_id=1, source_target_pairs={{0,8},{1,9},{2,10},{3,11},{4,12},{5,13},{6,14},{7,15},{8,0},{9,1},... | collective-permute-start | bytes 6291464 | tf_op jit(solution)/shard_map/inputs_exchange/ppermute | solution.py:114
  343.4 37.2 %all-to-all-start.1 = ((f32[8,256,128]{2,1,0:T(8,128)}), f32[8,256,128]{2,1,0:T(8,128)S(1)}, u32[]{:S(2)}, u32[]{:S(2)}) async-start(f32[8,256,128]{2,1,0:T(8,128)} %add.50), calls=%async_computation.1 | async-start | bytes 2097152 | tf_op jit(solution)/shard_map/to_owners/all_to_all | solution.py:124
  362.4 139.0 %collective-permute-start.6 = (f32[8,512,128]{2,1,0:T(8,128)S(1)}, f32[8,512,128]{2,1,0:T(8,128)}, u32[]{:S(2)}, u32[]{:S(2)}) collective-permute-start(f32[8,512,128]{2,1,0:T(8,128)S(1)} %shard_map.33), channel_id=1, source_target_pairs={{0,16},{1,17},{2,18},{3,19},{4,20},{5,21},{6,22},{7,23},{8,24},{9,... | collective-permute-start | bytes 6291464 | tf_op jit(solution)/shard_map/ppermute | solution.py:119
  380.6 123.9 %all-to-all-start.7 = ((f32[8,512,128]{2,1,0:T(8,128)}), f32[8,512,128]{2,1,0:T(8,128)}, u32[]{:S(2)}, u32[]{:S(2)}) async-start(f32[8,512,128]{2,1,0:T(8,128)} %add.53), calls=%async_computation.7 | async-start | bytes 4194304 | tf_op jit(solution)/shard_map/to_owners/all_to_all | solution.py:124
  400.9 145.4 %collective-permute-start.4 = (f32[8,512,128]{2,1,0:T(8,128)}, f32[8,512,128]{2,1,0:T(8,128)}, u32[]{:S(2)}, u32[]{:S(2)}) collective-permute-start(f32[8,512,128]{2,1,0:T(8,128)} %shard_map.31), channel_id=1, source_target_pairs={{0,16},{1,17},{2,18},{3,19},{4,20},{5,21},{6,22},{7,23},{8,24},{9,... | collective-permute-start | bytes 6291464 | tf_op jit(solution)/shard_map/ppermute | solution.py:119
  504.5 44.9 %all-to-all-start.5 = ((f32[8,512,128]{2,1,0:T(8,128)}), f32[8,512,128]{2,1,0:T(8,128)S(1)}, u32[]{:S(2)}, u32[]{:S(2)}) async-start(f32[8,512,128]{2,1,0:T(8,128)} %add.52), calls=%async_computation.5 | async-start | bytes 4194304 | tf_op jit(solution)/shard_map/to_owners/all_to_all | solution.py:124
Sparse Core Ops, SparseCore 0:
  41.3 89.1 all-gather.6
  132.3 92.2 all-gather.4

commit v2 on v1

--- a/solution.py
+++ b/solution.py
@@ -13,16 +13,22 @@
 VMEM_BYTES = 48 * 1024 * 1024
 
 
-def squares_kernel(near_ref, far_ref, grads_ref, out_ref, turned):
+def squares_kernel(per, near_ref, far_ref, grads_ref, *refs):
+    out_ref, turned = refs[-2:]
     seqs = near_ref.shape[0]
+    chips = seqs // (2 * per)
     tile_d = out_ref.shape[0] * out_ref.shape[2]
     owned = out_ref.shape[2]
 
     @pl.when(pl.program_id(1) == 0)
     def turn():
-        for s in range(seqs):
-            turned[2 * s] = near_ref[s].T
-            turned[2 * s + 1] = far_ref[s].T
+        for core in range(2):
+            for chip in range(chips):
+                for s in range(per):
+                    source = (chip * 2 + core) * per + s
+                    place = (core * chips + chip) * 2 * per + s
+                    turned[place] = near_ref[source].T
+                    turned[place + per] = far_ref[source].T
 
     start = pl.multiple_of(pl.program_id(1) * tile_d, tile_d)
     for half in range(tile_d // 256):
@@ -38,14 +44,15 @@
             out_ref[half * (256 // owned) + j] = total[:, j * owned:(j + 1) * owned]
 
 
-def squares(near, far, grads, owned):
+def squares(per, near, far, grads, owned, after):
     seqs, _, f = near.shape
     d = grads.shape[2]
     inputs = pl.BlockSpec((seqs, LEN, TILE_F), lambda i, j: (0, 0, i))
     return pl.pallas_call(
-        squares_kernel,
+        functools.partial(squares_kernel, per),
         grid=(f // TILE_F, d // TILE_D),
-        in_specs=[inputs, inputs, pl.BlockSpec((2 * seqs, LEN, d), lambda i, j: (0, 0, 0))],
+        in_specs=[inputs, inputs, pl.BlockSpec((2 * seqs, LEN, d), lambda i, j: (0, 0, 0))]
+        + [pl.BlockSpec(memory_space=pl.ANY)] * len(after),
         out_specs=pl.BlockSpec((TILE_D // owned, TILE_F, owned), lambda i, j: (j, i, 0)),
         out_shape=jax.ShapeDtypeStruct((d // owned, f, owned), jnp.float32),
         scratch_shapes=[pltpu.VMEM((2 * seqs, TILE_F, LEN), jnp.bfloat16)],
@@ -55,7 +62,7 @@
             bytes_accessed=2 * 2 * seqs * LEN * (f + d) + 4 * f * d,
             transcendentals=0,
         ),
-    )(near, far, grads)
+    )(near, far, grads, *after)
 
 
 def scattered(activations, gathered, n):
@@ -77,12 +84,14 @@
     inner, lo = 8, 2
     hi = n // (inner * lo)
     tiles = f // (inner * TILE_F)
-    if n % (inner * lo) or f % (inner * TILE_F) or owned != 128:
+    if n % (inner * lo) or hi < 2 or tiles < 3 or f % (inner * TILE_F) or owned != 128:
         return scattered(activations, gathered, n)
 
     me = lax.axis_index("dp")
     h, l = me // (inner * lo), (me // inner) % lo
     groups = [[k * inner + i for i in range(inner)] for k in range(n // inner)]
+    chips = [[k * inner + 2 * q + c for q in range(inner // 2)] for k in range(n // inner) for c in range(2)]
+    cores = [[2 * k, 2 * k + 1] for k in range(n // 2)]
     swap_lo = [(k, k ^ inner) for k in range(n)]
     step = inner * lo
 
@@ -96,14 +105,15 @@
         cols = []
         for shift in list(range(1, hi)) + [0]:
             part = lax.dynamic_index_in_dim(both, (h + shift) % hi, 2, keepdims=False)
-            part = part.reshape(2, seqs, LEN, inner * owned).transpose(1, 0, 2, 3)
-            part = lax.all_gather(part, "dp", axis_index_groups=groups)
+            part = part.reshape(2 * seqs, LEN, inner * owned)
+            part = lax.all_gather(part, "dp", axis_index_groups=chips, tiled=True)
+            part = lax.all_gather(part, "dp", axis_index_groups=cores, tiled=True)
             cols.append(part.reshape(inner * seqs * 2, LEN, inner * owned))
 
-    sizes = [1] + [2] * ((tiles - 1) // 2) + [1] * ((tiles - 1) % 2)
+    sizes = [1] + [2] * ((tiles - 3) // 2) + [1] * (tiles - 1 - 2 * ((tiles - 3) // 2))
     wide = f // inner
     a = activations.reshape(rows, inner, wide)
-    pieces = []
+    sources = []
     first = 0
     for size in sizes:
         chunk = a[:, :, first * TILE_F:(first + size) * TILE_F].transpose(1, 0, 2)
@@ -112,13 +122,23 @@
             near = lax.all_to_all(chunk, "dp", 0, 0, axis_index_groups=groups, tiled=True)
             near = near.reshape(inner * seqs, LEN, size * TILE_F)
             far = lax.ppermute(near, "dp", swap_lo)
-        arrived = []
+        sources.append((near, far))
+
+    sent, arrived = [], []
+    for near, far in sources:
+        landed = []
         for shift in range(1, hi):
-            part = squares(near, far, cols[shift - 1], owned)
+            part = squares(seqs, near, far, cols[shift - 1], owned, sent[-1:])
             pairs = [(k, (k + shift * step) % n) for k in range(n)]
-            arrived.append(lax.ppermute(part, "dp", pairs))
-        total = squares(near, far, cols[-1], owned)
-        for part in arrived:
+            sent.append(part)
+            landed.append(lax.ppermute(part, "dp", pairs))
+        arrived.append(landed)
+    pieces, total = [], None
+    for k, (near, far) in enumerate(sources):
+        after = [sent[min(k + 2, len(sources) - 1) * (hi - 1)]]
+        after += ([total] if k >= 1 else []) + ([pieces[k - 2]] if k >= 2 else [])
+        total = squares(seqs, near, far, cols[-1], owned, after)
+        for part in arrived[k]:
             total = total + part
         with jax.named_scope("to_owners"):
             pieces.append(lax.all_to_all(total, "dp", 0, 0, axis_index_groups=groups, tiled=True))

time: 598 us -> 735 us (1.23)
  waiting for transfers between devices: 329 us -> 464 us
  blocking collectives: 30.4 us -> 0 us
  starting transfers between devices: 45.6 us -> 59.1 us
  local copies, waits for them, and re-layouts: 45.6 us -> 56.9 us
  Pallas kernels: 109 us -> 117 us
    ppermute x4 -> x5, waiting for transfers between devices: 0.97 us -> 132 us  [per_device(): far = lax.ppermute(near, 'dp', swap_lo)]
    all_gather x2 -> x4, waiting for transfers between devices: 0.01 us -> 108 us  [the longest x2 108 us: per_device(): part = lax.all_gather(part, 'dp', axis_index_groups=chips, tiled=True)]
    ppermute x4 -> x5, waiting for transfers between devices: 204 us -> 139 us  [per_device(): landed.append(lax.ppermute(part, 'dp', pairs))]
    all_to_all x4 -> x5, waiting for transfers between devices: 101 us -> 55.6 us  [per_device(): lax.all_to_all(chunk, 'dp', 0, 0, axis_index_groups=groups, tiled=True)]
    all_to_all x1 -> x0, blocking collectives: 30.4 us -> none  [per_device(): lax.all_to_all(total, 'dp', 0, 0, axis_index_groups=groups, tiled=True)]
    unnamed x8 -> x54, local copies, waits for them, and re-layouts: 20.4 us -> 38.5 us
    all_gather x2 -> x0, local copies, waits for them, and re-layouts: 16.4 us -> none  [per_device(): part = lax.all_gather(part, 'dp', axis_index_groups=groups)]
    all_to_all x3 -> x5, starting transfers between devices: 12.5 us -> 21.4 us  [per_device(): lax.all_to_all(total, 'dp', 0, 0, axis_index_groups=groups, tiled=True)]
  transfers between devices with their start and end apart: 18 -> 25, of which waited for: 9 -> 13; matrix products, arithmetic and copies ran while one was open for 8% -> 6% of each run, Pallas kernels for 18% -> 16%
where the time goes in v2:
time: 735 us; the launch traced here: 725 us
  waiting for transfers between devices  464 us (63%)
  Pallas kernels  117 us (16%)
  starting transfers between devices  59.1 us (8%)
  local copies, waits for them, and re-layouts  56.9 us (8%)
  other arithmetic  14.7 us (2%)
  between operations  13.7 us (2%)
    ppermute x5, waiting for transfers between devices, per_device(): landed.append(lax.ppermute(part, 'dp', pairs))  139 us
    ppermute x5, waiting for transfers between devices, per_device(): far = lax.ppermute(near, 'dp', swap_lo)  132 us
    pallas_call x10, Pallas kernels, squares(): pl.pallas_call(functools.partial(squares_kernel, per), grid=(f // TILE_F,...  117 us
    all_gather x2, waiting for transfers between devices, per_device(): part = lax.all_gather(part, 'dp', axis_index_groups=chips, tiled=True)  108 us
    all_to_all x5, waiting for transfers between devices, per_device(): lax.all_to_all(chunk, 'dp', 0, 0, axis_index_groups=groups, tiled=True)  55.6 us
    unnamed x54, local copies, waits for them, and re-layouts  38.5 us
    ppermute x1, waiting for transfers between devices, per_device(): got = lax.ppermute(theirs, 'dp', swap_lo)  22.9 us
    all_to_all x5, starting transfers between devices, per_device(): lax.all_to_all(total, 'dp', 0, 0, axis_index_groups=groups, tiled=True)  21.4 us
  transfers between devices with their start and end apart: 25, of which 13 were waited for; matrix products, arithmetic and copies ran while one was open for 6% of the time, Pallas kernels for 16%

profile of v2, /device:TPU:0, one launch (start us, length us, event | category | flops | bytes accessed | tf_op | source)
XLA Modules:
  0.0 725.1 jit_solution(9119149398202580620)
XLA Ops:
  9.9 5.6 constant_dynamic-slice_fusion
  20.7 22.9 %collective-permute-done.1 = bf16[256,2,1024]{2,0,1:T(8,128)(2,1)} collective-permute-done((bf16[256,2,1024]{2,0,1:T(8,128)(2,1)}, bf16[256,2,1024]{2,0,1:T(8,128)(2,1)}, u32[]{:S(2)}, u32[]{:S(2)}) %collective-permute-start.1) | collective-permute-done | bytes 1048608 | tf_op jit(solution)/shard_map/grads_exchange/ppermute | solution.py:102
  47.1 53.5 %all-gather.9.cloned.1.call-done = bf16[16,128,1024]{2,1,0:T(8,128)(2,1)} async-done(((bf16[4,128,1024]{2,1,0:T(8,128)(2,1)}), bf16[16,128,1024]{2,1,0:T(8,128)(2,1)}) %all-gather.9.cloned.1.call-update) | async-done | bytes 4194320 | tf_op jit(solution)/shard_map/grads_exchange/all_gather | solution.py:109
  100.7 54.5 %all-gather.5.cloned.1.call-done = bf16[16,128,1024]{2,1,0:T(8,128)(2,1)} async-done(((bf16[4,128,1024]{2,1,0:T(8,128)(2,1)}), bf16[16,128,1024]{2,1,0:T(8,128)(2,1)}) %all-gather.5.cloned.1.call-update) | async-done | bytes 4194320 | tf_op jit(solution)/shard_map/grads_exchange/all_gather | solution.py:109
  155.2 5.2 copy.22
  169.9 4.8 fusion.3
  176.7 8.5 %all-to-all-done = bf16[8,256,256]{2,1,0:T(8,128)(2,1)S(1)} async-done(((bf16[8,256,256]{2,1,0:T(8,128)(2,1)}), bf16[8,256,256]{2,1,0:T(8,128)(2,1)S(1)}, u32[]{:S(2)}, u32[]{:S(2)}) %all-to-all-start) | async-done | bytes 1048608 | tf_op jit(solution)/shard_map/inputs_exchange/all_to_all | solution.py:122
  192.9 22.6 %all-to-all-done.2 = bf16[8,256,512]{2,1,0:T(8,128)(2,1)S(1)} async-done(((bf16[8,256,512]{2,1,0:T(8,128)(2,1)}), bf16[8,256,512]{2,1,0:T(8,128)(2,1)S(1)}, u32[]{:S(2)}, u32[]{:S(2)}) %all-to-all-start.2) | async-done | bytes 2097184 | tf_op jit(solution)/shard_map/inputs_exchange/all_to_all | solution.py:122
  222.8 24.5 %all-to-all-done.1 = bf16[8,256,512]{2,1,0:T(8,128)(2,1)S(1)} async-done(((bf16[8,256,512]{2,1,0:T(8,128)(2,1)}), bf16[8,256,512]{2,1,0:T(8,128)(2,1)S(1)}, u32[]{:S(2)}, u32[]{:S(2)}) %all-to-all-start.1) | async-done | bytes 2097184 | tf_op jit(solution)/shard_map/inputs_exchange/all_to_all | solution.py:122
  251.1 4.2 all-to-all-start.4
  255.3 36.6 %collective-permute-done.far_ref = bf16[16,128,256]{2,1,0:T(8,128)(2,1)} collective-permute-done((bf16[16,128,256]{2,1,0:T(8,128)(2,1)S(1)}, bf16[16,128,256]{2,1,0:T(8,128)(2,1)}, u32[]{:S(2)}, u32[]{:S(2)}) %collective-permute-start) | collective-permute-done | bytes 1048608 | tf_op jit(solution)/shard_map/inputs_exchange/ppermute | solution.py:124
  292.0 10.0 %shard_map.28.refs_0_ = f32[8,256,128]{2,1,0:T(8,128)} custom-call(bf16[16,128,256]{2,1,0:T(8,128)(2,1)S(1)} %bitcast.39, bf16[16,128,256]{2,1,0:T(8,128)(2,1)} %collective-permute-done.far_ref, bf16[32,128,1024]{2,1,0:T(8,128)(2,1)} %all-gather.11.cloned.1.call-done.grads_ref), custom_call_target="tpu_custom_call" | custom-call | flops 2147483648 | bytes 11534336 | tf_op jit(solution)/shard_map/pallas_call | solution.py:51
  302.0 15.6 %shard_map.29.refs_0_ = f32[8,512,128]{2,1,0:T(8,128)} custom-call(bf16[16,128,512]{2,1,0:T(8,128)(2,1)S(1)} %bitcast.43, bf16[16,128,512]{2,1,0:T(8,128)(2,1)} %collective-permute-done.3.far_ref, bf16[32,128,1024]{2,1,0:T(8,128)(2,1)} %all-gather.11.cloned.1.call-done.grads_ref, f32[8,256,128]{2,1,0:T(8,128)} %shard_map.28.refs_0_), custom_call_target="tpu_custom_call" | custom-call | flops 4294967296 | bytes 14680064 | tf_op jit(solution)/shard_map/pallas_call | solution.py:51
  321.7 4.5 all-to-all-start.6
  327.6 27.0 %collective-permute-done.2.far_ref = bf16[16,128,512]{2,1,0:T(8,128)(2,1)} collective-permute-done((bf16[16,128,512]{2,1,0:T(8,128)(2,1)S(1)}, bf16[16,128,512]{2,1,0:T(8,128)(2,1)}, u32[]{:S(2)}, u32[]{:S(2)}) %collective-permute-start.2) | collective-permute-done | bytes 2097184 | tf_op jit(solution)/shard_map/inputs_exchange/ppermute | solution.py:124
  354.6 14.8 %shard_map.30.refs_0_ = f32[8,512,128]{2,1,0:T(8,128)S(1)} custom-call(bf16[16,128,512]{2,1,0:T(8,128)(2,1)S(1)} %bitcast.33, bf16[16,128,512]{2,1,0:T(8,128)(2,1)} %collective-permute-done.2.far_ref, bf16[32,128,1024]{2,1,0:T(8,128)(2,1)} %all-gather.11.cloned.1.call-done.grads_ref, f32[8,512,128]{2,1,0:T(8,128)} %shard_map.29.refs_0_), custom_call_target="tpu_custom_call" | custom-call | flops 4294967296 | bytes 14680064 | tf_op jit(solution)/shard_map/pallas_call | solution.py:51
  373.5 9.1 %shard_map.31 = f32[8,256,128]{2,1,0:T(8,128)S(1)} custom-call(bf16[16,128,256]{2,1,0:T(8,128)(2,1)S(1)} %bitcast.40, bf16[16,128,256]{2,1,0:T(8,128)(2,1)} %collective-permute-done.far_ref, bf16[32,128,1024]{2,1,0:T(8,128)(2,1)} %all-gather.7.cloned.1.call-done.grads_ref, f32[8,512,128]{2,1,0:T(8,128)S(1)} %copy-done.2), custom_call_target="tpu_custom_call" | custom-call | flops 2147483648 | bytes 11534336 | tf_op jit(solution)/shard_map/pallas_call | solution.py:51
  382.6 72.8 %collective-permute-done.4 = f32[8,256,128]{2,1,0:T(8,128)} collective-permute-done((f32[8,256,128]{2,1,0:T(8,128)}, f32[8,256,128]{2,1,0:T(8,128)}, u32[]{:S(2)}, u32[]{:S(2)}) %collective-permute-start.4) | collective-permute-done | bytes 1048608 | tf_op jit(solution)/shard_map/ppermute | solution.py:134
  458.8 4.0 all-to-all-start.3
  462.9 9.5 %shard_map.32.refs_0_ = f32[8,256,128]{2,1,0:T(8,128)S(1)} custom-call(bf16[16,128,256]{2,1,0:T(8,128)(2,1)} %bitcast.12.near_ref, bf16[16,128,256]{2,1,0:T(8,128)(2,1)} %collective-permute-done.5.far_ref, bf16[32,128,1024]{2,1,0:T(8,128)(2,1)} %all-gather.11.cloned.1.call-done.grads_ref, f32[8,512,128]{2,1,0:T(8,128)S(1)} %copy-done.3), custom_call_target="tpu_custom_call" | custom-call | flops 2147483648 | bytes 11534336 | tf_op jit(solution)/shard_map/pallas_call | solution.py:51
  472.4 15.3 %shard_map.33 = f32[8,512,128]{2,1,0:T(8,128)S(1)} custom-call(bf16[16,128,512]{2,1,0:T(8,128)(2,1)} %bitcast.42, bf16[16,128,512]{2,1,0:T(8,128)(2,1)} %collective-permute-done.3.far_ref, bf16[32,128,1024]{2,1,0:T(8,128)(2,1)} %all-gather.7.cloned.1.call-done.grads_ref, f32[8,256,128]{2,1,0:T(8,128)S(1)} %shard_map.32.refs_0_, f32[8,256,128]{2,1,0:T(8,128)} %add.53.refs_1_), custom_call_target="tpu_custom_call" | custom-call | flops 4294967296 | bytes 14680064 | tf_op jit(solution)/shard_map/pallas_call | solution.py:51
  491.8 4.5 all-to-all-start.5
  500.2 68.2 %collective-permute-done.7.far_ref = bf16[16,128,256]{2,1,0:T(8,128)(2,1)S(1)} collective-permute-done((bf16[16,128,256]{2,1,0:T(8,128)(2,1)}, bf16[16,128,256]{2,1,0:T(8,128)(2,1)S(1)}, u32[]{:S(2)}, u32[]{:S(2)}) %collective-permute-start.7) | collective-permute-done | bytes 1048608 | tf_op jit(solution)/shard_map/inputs_exchange/ppermute | solution.py:124
  570.8 9.1 %shard_map.34.refs_0_ = f32[8,256,128]{2,1,0:T(8,128)S(1)} custom-call(bf16[16,128,256]{2,1,0:T(8,128)(2,1)S(1)} %bitcast.36, bf16[16,128,256]{2,1,0:T(8,128)(2,1)S(1)} %collective-permute-done.7.far_ref, bf16[32,128,1024]{2,1,0:T(8,128)(2,1)} %all-gather.11.cloned.1.call-done.grads_ref, f32[8,256,128]{2,1,0:T(8,128)S(1)} %copy-done.8), custom_call_target="tpu_custom_call" | custom-call | flops 2147483648 | bytes 11534336 | tf_op jit(solution)/shard_map/pallas_call | solution.py:51
  580.0 15.0 %shard_map.35 = f32[8,512,128]{2,1,0:T(8,128)S(1)} custom-call(bf16[16,128,512]{2,1,0:T(8,128)(2,1)} %bitcast.34, bf16[16,128,512]{2,1,0:T(8,128)(2,1)} %collective-permute-done.2.far_ref, bf16[32,128,1024]{2,1,0:T(8,128)(2,1)} %all-gather.7.cloned.1.call-done.grads_ref, f32[8,256,128]{2,1,0:T(8,128)S(1)} %shard_map.34.refs_0_, f32[8,512,128]{2,1,0:T(8,128)} %add.54.refs_1_, ...), custom_call_target="tpu_custom_call" | custom-call | flops 4294967296 | bytes 14680064 | tf_op jit(solution)/shard_map/pallas_call | solution.py:51
  598.2 4.5 all-to-all-start.7
  605.7 9.4 %shard_map.36 = f32[8,256,128]{2,1,0:T(8,128)S(1)} custom-call(bf16[16,128,256]{2,1,0:T(8,128)(2,1)} %bitcast.12.near_ref, bf16[16,128,256]{2,1,0:T(8,128)(2,1)} %collective-permute-done.5.far_ref, bf16[32,128,1024]{2,1,0:T(8,128)(2,1)} %all-gather.7.cloned.1.call-done.grads_ref, f32[8,256,128]{2,1,0:T(8,128)S(1)} %shard_map.34.refs_0_, ...), custom_call_target="tpu_custom_call" | custom-call | flops 2147483648 | bytes 11534336 | tf_op jit(solution)/shard_map/pallas_call | solution.py:51
  615.1 58.1 %collective-permute-done.9 = f32[8,256,128]{2,1,0:T(8,128)S(1)} collective-permute-done((f32[8,256,128]{2,1,0:T(8,128)S(1)}, f32[8,256,128]{2,1,0:T(8,128)S(1)}, u32[]{:S(2)}, u32[]{:S(2)}) %collective-permute-start.9) | collective-permute-done | bytes 1048608 | tf_op jit(solution)/shard_map/ppermute | solution.py:134
  674.3 4.5 all-to-all-start.8
  678.7 8.8 %shard_map.37 = f32[8,256,128]{2,1,0:T(8,128)S(1)} custom-call(bf16[16,128,256]{2,1,0:T(8,128)(2,1)S(1)} %bitcast.37, bf16[16,128,256]{2,1,0:T(8,128)(2,1)S(1)} %copy-done.18, bf16[32,128,1024]{2,1,0:T(8,128)(2,1)} %all-gather.7.cloned.1.call-done.grads_ref, f32[8,256,128]{2,1,0:T(8,128)S(1)} %shard_map.34.refs_0_, f32[8,256,128]{2,1,0:T(8,128)} %add.56.refs_1_, ...), custom_call_target="tpu_custom_call" | custom-call | flops 2147483648 | bytes 11534336 | tf_op jit(solution)/shard_map/pallas_call | solution.py:51
  687.5 8.2 %collective-permute-done.10 = f32[8,256,128]{2,1,0:T(8,128)} collective-permute-done((f32[8,256,128]{2,1,0:T(8,128)S(1)}, f32[8,256,128]{2,1,0:T(8,128)}, u32[]{:S(2)}, u32[]{:S(2)}) %collective-permute-start.10) | collective-permute-done | bytes 1048608 | tf_op jit(solution)/shard_map/ppermute | solution.py:134
  711.3 6.0 all-to-all-done.9
  (99 shorter events, 89.7 us)
Async XLA Ops:
  6.5 94.1 %all-gather.9.cloned.1.call-start = ((), (), s32[]{:S(2)}) async-start(), calls=%async_computation.12 | async-start | bytes 5242880 | tf_op jit(solution)/shard_map/grads_exchange/all_gather | solution.py:109
  17.1 26.5 %collective-permute-start.1 = (bf16[256,2,1024]{2,0,1:T(8,128)(2,1)}, bf16[256,2,1024]{2,0,1:T(8,128)(2,1)}, u32[]{:S(2)}, u32[]{:S(2)}) collective-permute-start(bf16[256,2,1024]{2,0,1:T(8,128)(2,1)} %bitcast.30), channel_id=1, source_target_pairs={{0,8},{1,9},{2,10},{3,11},{4,12},{5,13},{6,14},{7,15},{8,0},{9,1},... | collective-permute-start | bytes 3145736 | tf_op jit(solution)/shard_map/grads_exchange/ppermute | solution.py:102
  46.3 108.9 %all-gather.5.cloned.1.call-start = ((), (), s32[]{:S(2)}) async-start(), calls=%async_computation.10 | async-start | bytes 5242880 | tf_op jit(solution)/shard_map/grads_exchange/all_gather | solution.py:109
  47.1 244.9 %all-gather.11.cloned.1.call-start = ((), (), s32[]{:S(2)}) async-start(), calls=%async_computation.13 | async-start | bytes 12582912 | tf_op jit(solution)/shard_map/grads_exchange/all_gather | solution.py:110
  100.6 270.1 %all-gather.7.cloned.1.call-start = ((), (), s32[]{:S(2)}) async-start(), calls=%async_computation.11 | async-start | bytes 12582912 | tf_op jit(solution)/shard_map/grads_exchange/all_gather | solution.py:110
  166.2 19.0 %all-to-all-start = ((bf16[8,256,256]{2,1,0:T(8,128)(2,1)}), bf16[8,256,256]{2,1,0:T(8,128)(2,1)S(1)}, u32[]{:S(2)}, u32[]{:S(2)}) async-start(bf16[8,256,256]{2,1,0:T(8,128)(2,1)} %bitcast.29), calls=%async_computation | async-start | bytes 2097152 | tf_op jit(solution)/shard_map/inputs_exchange/all_to_all | solution.py:122
  185.2 106.8 %copy-start.13 = (bf16[8,256,256]{2,1,0:T(8,128)(2,1)}, bf16[8,256,256]{2,1,0:T(8,128)(2,1)S(1)}, u32[]{:S(2)}) copy-start(bf16[8,256,256]{2,1,0:T(8,128)(2,1)S(1)} %all-to-all-done) | copy-start | bytes 3145732
  185.2 30.2 %all-to-all-start.2 = ((bf16[8,256,512]{2,1,0:T(8,128)(2,1)}), bf16[8,256,512]{2,1,0:T(8,128)(2,1)S(1)}, u32[]{:S(2)}, u32[]{:S(2)}) async-start(bf16[8,256,512]{2,1,0:T(8,128)(2,1)} %bitcast.47), calls=%async_computation.2 | async-start | bytes 4194304 | tf_op jit(solution)/shard_map/inputs_exchange/all_to_all | solution.py:122
  216.9 30.4 %all-to-all-start.1 = ((bf16[8,256,512]{2,1,0:T(8,128)(2,1)}), bf16[8,256,512]{2,1,0:T(8,128)(2,1)S(1)}, u32[]{:S(2)}, u32[]{:S(2)}) async-start(bf16[8,256,512]{2,1,0:T(8,128)(2,1)} %bitcast.46), calls=%async_computation.1 | async-start | bytes 4194304 | tf_op jit(solution)/shard_map/inputs_exchange/all_to_all | solution.py:122
  220.7 81.3 %collective-permute-start.3 = (bf16[16,128,512]{2,1,0:T(8,128)(2,1)}, bf16[16,128,512]{2,1,0:T(8,128)(2,1)}, u32[]{:S(2)}, u32[]{:S(2)}) collective-permute-start(bf16[16,128,512]{2,1,0:T(8,128)(2,1)} %bitcast.41), channel_id=1, source_target_pairs={{0,8},{1,9},{2,10},{3,11},{4,12},{5,13},{6,14},{7,15},{8,0},{9,1},... | collective-permute-start | bytes 6291464 | tf_op jit(solution)/shard_map/inputs_exchange/ppermute | solution.py:124
  222.1 69.8 %collective-permute-start = (bf16[16,128,256]{2,1,0:T(8,128)(2,1)S(1)}, bf16[16,128,256]{2,1,0:T(8,128)(2,1)}, u32[]{:S(2)}, u32[]{:S(2)}) collective-permute-start(bf16[16,128,256]{2,1,0:T(8,128)(2,1)S(1)} %bitcast.38), channel_id=1, source_target_pairs={{0,8},{1,9},{2,10},{3,11},{4,12},{5,13},{6,14},{7,15},{8,0},{9,1},... | collective-permute-start | bytes 3145736 | tf_op jit(solution)/shard_map/inputs_exchange/ppermute | solution.py:124
  247.2 107.3 %copy-start = (bf16[8,256,512]{2,1,0:T(8,128)(2,1)}, bf16[8,256,512]{2,1,0:T(8,128)(2,1)S(1)}, u32[]{:S(2)}) copy-start(bf16[8,256,512]{2,1,0:T(8,128)(2,1)S(1)} %all-to-all-done.1) | copy-start | bytes 6291460
  247.3 107.3 %collective-permute-start.2 = (bf16[16,128,512]{2,1,0:T(8,128)(2,1)S(1)}, bf16[16,128,512]{2,1,0:T(8,128)(2,1)}, u32[]{:S(2)}, u32[]{:S(2)}) collective-permute-start(bf16[16,128,512]{2,1,0:T(8,128)(2,1)S(1)} %bitcast.32), channel_id=1, source_target_pairs={{0,8},{1,9},{2,10},{3,11},{4,12},{5,13},{6,14},{7,15},{8,0},{9,1},... | collective-permute-start | bytes 6291464 | tf_op jit(solution)/shard_map/inputs_exchange/ppermute | solution.py:124
  251.1 70.6 %all-to-all-start.4 = ((bf16[8,256,256]{2,1,0:T(8,128)(2,1)}), bf16[8,256,256]{2,1,0:T(8,128)(2,1)}, u32[]{:S(2)}, u32[]{:S(2)}) async-start(bf16[8,256,256]{2,1,0:T(8,128)(2,1)} %bitcast.53), calls=%async_computation.4 | async-start | bytes 2097152 | tf_op jit(solution)/shard_map/inputs_exchange/all_to_all | solution.py:122
  302.0 18.5 %copy-start.21 = (bf16[256,8,256]{2,1,0:T(8,128)(2,1)S(1)}, bf16[256,8,256]{2,1,0:T(8,128)(2,1)}, u32[]{:S(2)}) copy-start(bf16[256,8,256]{2,1,0:T(8,128)(2,1)} %get-tuple-element.5) | copy-start | bytes 3145732
  317.6 170.2 %collective-permute-start.6 = (f32[8,512,128]{2,1,0:T(8,128)}, f32[8,512,128]{2,1,0:T(8,128)}, u32[]{:S(2)}, u32[]{:S(2)}) collective-permute-start(f32[8,512,128]{2,1,0:T(8,128)} %shard_map.29.refs_0_), channel_id=1, source_target_pairs={{0,16},{1,17},{2,18},{3,19},{4,20},{5,21},{6,22},{7,23},{8,24},{9,... | collective-permute-start | bytes 6291464 | tf_op jit(solution)/shard_map/ppermute | solution.py:134
  319.9 135.6 %collective-permute-start.4 = (f32[8,256,128]{2,1,0:T(8,128)}, f32[8,256,128]{2,1,0:T(8,128)}, u32[]{:S(2)}, u32[]{:S(2)}) collective-permute-start(f32[8,256,128]{2,1,0:T(8,128)} %shard_map.28.refs_0_), channel_id=1, source_target_pairs={{0,16},{1,17},{2,18},{3,19},{4,20},{5,21},{6,22},{7,23},{8,24},{9,... | collective-permute-start | bytes 3145736 | tf_op jit(solution)/shard_map/ppermute | solution.py:134
  321.7 136.1 %all-to-all-start.6 = ((bf16[8,256,256]{2,1,0:T(8,128)(2,1)}), bf16[8,256,256]{2,1,0:T(8,128)(2,1)S(1)}, u32[]{:S(2)}, u32[]{:S(2)}) async-start(bf16[8,256,256]{2,1,0:T(8,128)(2,1)} %bitcast.52), calls=%async_computation.6 | async-start | bytes 2097152 | tf_op jit(solution)/shard_map/inputs_exchange/all_to_all | solution.py:122
  326.2 136.8 %collective-permute-start.5 = (bf16[16,128,256]{2,1,0:T(8,128)(2,1)}, bf16[16,128,256]{2,1,0:T(8,128)(2,1)}, u32[]{:S(2)}, u32[]{:S(2)}) collective-permute-start(bf16[16,128,256]{2,1,0:T(8,128)(2,1)} %bitcast.12.near_ref), channel_id=1, source_target_pairs={{0,8},{1,9},{2,10},{3,11},{4,12},{5,13},{6,14},{7,15},{8,0},{9,1},... | collective-permute-start | bytes 3145736 | tf_op jit(solution)/shard_map/inputs_exchange/ppermute | solution.py:124
  382.6 80.2 %copy-start.3 = (f32[8,512,128]{2,1,0:T(8,128)S(1)}, f32[8,512,128]{2,1,0:T(8,128)}, u32[]{:S(2)}) copy-start(f32[8,512,128]{2,1,0:T(8,128)} %copy-done.1) | copy-start | bytes 6291460
  458.8 32.1 %all-to-all-start.3 = ((f32[8,256,128]{2,1,0:T(8,128)}), f32[8,256,128]{2,1,0:T(8,128)S(1)}, u32[]{:S(2)}, u32[]{:S(2)}) async-start(f32[8,256,128]{2,1,0:T(8,128)} %add.53.refs_1_), calls=%async_computation.3 | async-start | bytes 2097152 | tf_op jit(solution)/shard_map/to_owners/all_to_all | solution.py:144
  462.8 132.2 %collective-permute-start.8 = (f32[8,512,128]{2,1,0:T(8,128)S(1)}, f32[8,512,128]{2,1,0:T(8,128)}, u32[]{:S(2)}, u32[]{:S(2)}) collective-permute-start(f32[8,512,128]{2,1,0:T(8,128)S(1)} %copy-done.3), channel_id=1, source_target_pairs={{0,16},{1,17},{2,18},{3,19},{4,20},{5,21},{6,22},{7,23},{8,24},{9,... | collective-permute-start | bytes 6291464 | tf_op jit(solution)/shard_map/ppermute | solution.py:134
  472.4 15.3 %copy-start.7 = (f32[8,256,128]{2,1,0:T(8,128)}, f32[8,256,128]{2,1,0:T(8,128)S(1)}, u32[]{:S(2)}) copy-start(f32[8,256,128]{2,1,0:T(8,128)S(1)} %shard_map.32.refs_0_) | copy-start | bytes 3145732
  491.8 106.3 %all-to-all-start.5 = ((f32[8,512,128]{2,1,0:T(8,128)}), f32[8,512,128]{2,1,0:T(8,128)}, u32[]{:S(2)}, u32[]{:S(2)}) async-start(f32[8,512,128]{2,1,0:T(8,128)} %add.54.refs_1_), calls=%async_computation.5 | async-start | bytes 4194304 | tf_op jit(solution)/shard_map/to_owners/all_to_all | solution.py:144
  496.4 83.6 %copy-start.5 = (f32[8,256,128]{2,1,0:T(8,128)S(1)}, f32[8,256,128]{2,1,0:T(8,128)}, u32[]{:S(2)}) copy-start(f32[8,256,128]{2,1,0:T(8,128)} %copy-done.4) | copy-start | bytes 3145732
  496.4 72.0 %collective-permute-start.7 = (bf16[16,128,256]{2,1,0:T(8,128)(2,1)}, bf16[16,128,256]{2,1,0:T(8,128)(2,1)S(1)}, u32[]{:S(2)}, u32[]{:S(2)}) collective-permute-start(bf16[16,128,256]{2,1,0:T(8,128)(2,1)} %bitcast.35), channel_id=1, source_target_pairs={{0,8},{1,9},{2,10},{3,11},{4,12},{5,13},{6,14},{7,15},{8,0},{9,1},... | collective-permute-start | bytes 3145736 | tf_op jit(solution)/shard_map/inputs_exchange/ppermute | solution.py:124
  598.2 76.1 %all-to-all-start.7 = ((f32[8,512,128]{2,1,0:T(8,128)}), f32[8,512,128]{2,1,0:T(8,128)}, u32[]{:S(2)}, u32[]{:S(2)}) async-start(f32[8,512,128]{2,1,0:T(8,128)} %add.55.refs_1_), calls=%async_computation.7 | async-start | bytes 4194304 | tf_op jit(solution)/shard_map/to_owners/all_to_all | solution.py:144
  602.7 70.5 %collective-permute-start.9 = (f32[8,256,128]{2,1,0:T(8,128)S(1)}, f32[8,256,128]{2,1,0:T(8,128)S(1)}, u32[]{:S(2)}, u32[]{:S(2)}) collective-permute-start(f32[8,256,128]{2,1,0:T(8,128)S(1)} %copy-done.9), channel_id=1, source_target_pairs={{0,16},{1,17},{2,18},{3,19},{4,20},{5,21},{6,22},{7,23},{8,24},{9,... | collective-permute-start | bytes 3145736 | tf_op jit(solution)/shard_map/ppermute | solution.py:134
  602.7 92.9 %collective-permute-start.10 = (f32[8,256,128]{2,1,0:T(8,128)S(1)}, f32[8,256,128]{2,1,0:T(8,128)}, u32[]{:S(2)}, u32[]{:S(2)}) collective-permute-start(f32[8,256,128]{2,1,0:T(8,128)S(1)} %shard_map.34.refs_0_), channel_id=1, source_target_pairs={{0,16},{1,17},{2,18},{3,19},{4,20},{5,21},{6,22},{7,23},{8,24},{9,... | collective-permute-start | bytes 3145736 | tf_op jit(solution)/shard_map/ppermute | solution.py:134
  615.1 63.6 %copy-start.12 = (bf16[8,256,256]{2,1,0:T(8,128)(2,1)S(1)}, bf16[8,256,256]{2,1,0:T(8,128)(2,1)}, u32[]{:S(2)}) copy-start(bf16[8,256,256]{2,1,0:T(8,128)(2,1)} %copy-done.10) | copy-start | bytes 3145732
  674.3 23.8 %all-to-all-start.8 = ((f32[8,256,128]{2,1,0:T(8,128)}), f32[8,256,128]{2,1,0:T(8,128)}, u32[]{:S(2)}, u32[]{:S(2)}) async-start(f32[8,256,128]{2,1,0:T(8,128)} %add.56.refs_1_), calls=%async_computation.8 | async-start | bytes 2097152 | tf_op jit(solution)/shard_map/to_owners/all_to_all | solution.py:144
  698.0 19.3 %all-to-all-start.9 = ((f32[8,256,128]{2,1,0:T(8,128)}), f32[8,256,128]{2,1,0:T(8,128)S(1)}, u32[]{:S(2)}, u32[]{:S(2)}) async-start(f32[8,256,128]{2,1,0:T(8,128)} %add.57), calls=%async_computation.9 | async-start | bytes 2097152 | tf_op jit(solution)/shard_map/to_owners/all_to_all | solution.py:144
  (15 other events, 61.3 us)
Sparse Core Ops, SparseCore 0:
  46.4 54.1 all-gather.8
  102.4 52.6 all-gather.4
  156.7 19.8 all-gather.10
  178.0 21.0 all-gather.6
